TPU v7x, 512 devices: a whole 4x8x8 slice. The times are simulated.
512 devices in a mesh: seq: 128 (over z_lo, x, y), dp: 4 (over z_hi, core).
Axes of the slice: x: 4, y: 8, z: 8 (z_hi: 2, z_lo: 4; z = z_hi * 4 + z_lo), core: 2. Of those that a mesh axis runs over, the one named last changes fastest.
Arguments:
- byte_qkv: bfloat16 [4, 32768, 3072], P('dp', 'seq'), may hold values from -6 to 6
- patch_qkv: bfloat16 [4, 8192, 3072], P('dp', 'seq'), may hold values from -6 to 6
- patch_gain: float32 [3072], replicated, may hold values from 0.3 to 1.5
- out_grad: bfloat16 [4, 32768, 1024], P('dp', 'seq'), may hold values from -48 to 48
- patch_slot: int32 [4, 32768], P('dp', 'seq'), may hold values from 0 to 63, as said below
- lead: int32 [4, 128], P('dp', 'seq'), may hold values from 0 to 15, as said below
Outputs:
- byte_grad: bfloat16 [4, 32768, 3072], P('dp', 'seq')
- patch_grad: bfloat16 [4, 8192, 3072], P('dp', 'seq')
- gain_grad: float32 [3072], replicated
Inputs may be any that keep to these rules, and one draw needn't show every extreme that they name: Patches are runs of 1 to 31 bytes of a stream. A patch is owned by the device that holds its first byte; each device numbers the patches starting on it 0, 1, 2 and so on in order, and patch_slot gives each byte the number of its patch on the owning device. Every device holds the first byte of at least one patch. lead[s, d] bytes at the start of device d's run of stream s belong to the last patch that starts on device d - 1; lead[s, 0] = 0.
All inputs are finite; a program needn't handle non-finite values.
Results may differ from a plain program's by a relative error of at most 0.011.
Values may be sent and summed in bfloat16 or wider, within the bound.
A program may use at most 128 MiB of HBM per device.

v0:
```python
import math
import jax
import jax.numpy as jnp
from jax import lax
from jax.sharding import PartitionSpec as P

HEADS = 8
HEAD_DIM = 128
WIN = 512


def shifted(value, axis, steps):
    count = lax.axis_size(axis)
    initial, last = (max(0, -steps), min(count, count - steps))
    return lax.ppermute(value, axis, [(source, source + steps) for source in range(initial, last)])


def local(byte_qkv, patch_qkv, patch_gain, out_grad, patch_slot, lead):
    own_bytes = byte_qkv[0]
    patch_table = patch_qkv[0]
    cotangent = out_grad[0]
    slot_ids = patch_slot[0]
    row_count = own_bytes.shape[0]
    feature_count = cotangent.shape[1]
    capacity = patch_table.shape[0]
    first_pos = lax.axis_index("seq") * row_count
    reach_blocks = -(-WIN // row_count)
    inv_sqrt = 1.0 / math.sqrt(HEAD_DIM)
    local_rows = lax.broadcasted_iota(jnp.int32, (row_count,), 0)
    leading = local_rows < lead[0, 0]
    owned_slots = jnp.where(leading, -1, slot_ids)
    last_slot = jnp.max(owned_slots)
    last_row = lax.dynamic_slice_in_dim(patch_table, last_slot, 1, 0)
    prev_row = shifted(last_row, "seq", 1)
    slot_axis = lax.broadcasted_iota(jnp.int32, (row_count, capacity), 1)
    pick_rows = (slot_ids[:, None] == slot_axis).astype(jnp.bfloat16)
    patch_rows = jnp.dot(pick_rows, patch_table, preferred_element_type=jnp.float32)
    patch_rows = jnp.where(leading[:, None], prev_row.astype(jnp.float32), patch_rows)
    hidden = (patch_gain * patch_rows + own_bytes.astype(jnp.float32)).astype(jnp.bfloat16)
    queries = hidden[:, :feature_count]
    key_values = hidden[:, feature_count:]
    blocks = [key_values]
    arrived = shifted(key_values, "seq", 1)
    blocks.append(arrived)
    steps_back = 2
    arrived = shifted(key_values, "seq", steps_back)
    blocks.append(arrived)
    window = jnp.concatenate(blocks[::-1], axis=0)
    key_count = window.shape[0]
    query_pos = first_pos + local_rows
    key_pos = (
        first_pos - reach_blocks * row_count + lax.broadcasted_iota(jnp.int32, (key_count,), 0)
    )
    in_window = (
        (key_pos[None, :] <= query_pos[:, None])
        & (key_pos[None, :] > query_pos[:, None] - WIN)
        & (key_pos[None, :] >= 0)
    )
    query_parts = []
    key_parts = []
    value_parts = []
    max_list = []
    total_list = []
    delta_list = []
    for head_index in range(HEADS):
        low = head_index * HEAD_DIM
        query_head = queries[:, low : low + HEAD_DIM]
        cot_head = cotangent[:, low : low + HEAD_DIM]
        key_head = window[:, low : low + HEAD_DIM]
        value_head = window[:, feature_count + low : feature_count + low + HEAD_DIM]
        scores = (
            jnp.einsum("qe,ke->qk", query_head, key_head, preferred_element_type=jnp.float32)
            * inv_sqrt
        )
        scores = jnp.where(in_window, scores, -jnp.inf)
        row_max = jnp.max(scores, axis=1, keepdims=True)
        exponent = jnp.where(in_window, jnp.exp(scores - row_max), 0.0)
        row_total = jnp.sum(exponent, axis=1, keepdims=True)
        attn_prob = exponent / row_total
        prob_half = attn_prob.astype(jnp.bfloat16)
        value_parts.append(
            jnp.einsum("qk,qe->ke", prob_half, cot_head, preferred_element_type=jnp.float32)
        )
        prob_grad = jnp.einsum(
            "qe,ke->qk", cot_head, value_head, preferred_element_type=jnp.float32
        )
        row_delta = jnp.sum(attn_prob * prob_grad, axis=1, keepdims=True)
        score_grad = (attn_prob * (prob_grad - row_delta)).astype(jnp.bfloat16)
        query_parts.append(
            jnp.einsum("qk,ke->qe", score_grad, key_head, preferred_element_type=jnp.float32)
            * inv_sqrt
        )
        key_parts.append(
            jnp.einsum("qk,qe->ke", score_grad, query_head, preferred_element_type=jnp.float32)
            * inv_sqrt
        )
        max_list.append(row_max[:, 0])
        total_list.append(row_total[:, 0])
        delta_list.append(row_delta[:, 0])
    query_grad = jnp.concatenate(query_parts, axis=1)
    key_part = jnp.concatenate(key_parts, axis=1)
    value_part = jnp.concatenate(value_parts, axis=1)
    back_grads = jnp.concatenate([key_part, value_part], axis=1)
    own_grads = back_grads[key_count - row_count :]
    for steps_back in range(1, reach_blocks + 1):
        piece_first = (reach_blocks - steps_back) * row_count
        piece = back_grads[piece_first : piece_first + row_count]
        own_grads = own_grads + shifted(piece, "seq", -steps_back)
    hidden_grad = jnp.concatenate([query_grad, own_grads], axis=1)
    byte_grad = hidden_grad.astype(jnp.bfloat16)[None]
    lead_sum = jnp.sum(jnp.where(leading[:, None], hidden_grad, 0.0), axis=0, keepdims=True)
    from_next = shifted(lead_sum, "seq", -1)
    slot_column = lax.broadcasted_iota(jnp.int32, (capacity, row_count), 0)
    member = ((slot_ids[None, :] == slot_column) & jnp.logical_not(leading)[None, :]).astype(
        jnp.float32
    )
    slot_sums = jnp.dot(
        member, hidden_grad, precision=lax.Precision.HIGHEST, preferred_element_type=jnp.float32
    )
    slot_index = lax.broadcasted_iota(jnp.int32, (capacity, 1), 0)
    slot_sums = slot_sums + (slot_index == last_slot).astype(jnp.float32) * from_next
    patch_grad = (patch_gain * slot_sums).astype(jnp.bfloat16)[None]
    gain_term = jnp.sum(slot_sums * patch_table.astype(jnp.float32), axis=0)
    gain_grad = lax.psum(gain_term, ("seq", "dp")) / row_count
    return (byte_grad, patch_grad, gain_grad)


def solution(mesh):
    placed = (
        P("dp", "seq", None),
        P("dp", "seq", None),
        P(),
        P("dp", "seq", None),
        P("dp", "seq"),
        P("dp", "seq"),
    )
    return jax.shard_map(
        local,
        mesh=mesh,
        in_specs=placed,
        out_specs=(P("dp", "seq", None), P("dp", "seq", None), P()),
        check_vma=False,
    )
```

profile of v0, /device:TPU:1, one launch (start us, length us, event | category | flops | bytes accessed | tf_op | source)
XLA Modules:
  0.0 348.9 jit_solution(16617319942461404328)
XLA Ops:
  1.3 1.3 select_reduce_fusion.1
  4.5 0.8 dynamic-slice_bitcast_fusion
  5.4 4.0 %collective-permute-start = (bf16[1,3072]{1,0:T(2,128)(2,1)S(1)}, bf16[1,3072]{1,0:T(2,128)(2,1)S(1)}, u32[]{:S(2)}, u32[]{:S(2)}) collective-permute-start(bf16[1,3072]{1,0:T(2,128)(2,1)S(1)} %dynamic-slice_bitcast_fusion), channel_id=1, source_target_pairs={{0,4},{4,8},{8,12},{12,16},{16,20},{20,24},{24,28},{28,32},{32,36}... | collective-permute-start | bytes 18440 | tf_op jit(solution)/shard_map/ppermute | solution.py:15
  9.4 0.8 collective-permute-done
  10.2 2.3 fusion
  12.6 4.6 %collective-permute-start.2 = (bf16[256,2048]{1,0:T(8,128)(2,1)S(1)}, bf16[256,2048]{1,0:T(8,128)(2,1)}, u32[]{:S(2)}, u32[]{:S(2)}) collective-permute-start(bf16[256,2048]{1,0:T(8,128)(2,1)S(1)} %slice.154), channel_id=1, source_target_pairs={{0,4},{4,8},{8,12},{12,16},{16,20},{20,24},{24,28},{28,32},{32,36}... | collective-permute-start | bytes 3145736 | tf_op jit(solution)/shard_map/ppermute | solution.py:15
  17.2 5.1 %collective-permute-start.1 = (bf16[256,2048]{1,0:T(8,128)(2,1)S(1)}, bf16[256,2048]{1,0:T(8,128)(2,1)}, u32[]{:S(2)}, u32[]{:S(2)}) collective-permute-start(bf16[256,2048]{1,0:T(8,128)(2,1)S(1)} %slice.154), channel_id=1, source_target_pairs={{0,8},{4,12},{8,16},{12,20},{16,24},{20,28},{24,32},{28,36},{32,40... | collective-permute-start | bytes 3145736 | tf_op jit(solution)/shard_map/ppermute | solution.py:15
  22.3 0.6 compare_convert_fusion
  23.0 10.7 %collective-permute-done.2 = bf16[256,2048]{1,0:T(8,128)(2,1)} collective-permute-done((bf16[256,2048]{1,0:T(8,128)(2,1)S(1)}, bf16[256,2048]{1,0:T(8,128)(2,1)}, u32[]{:S(2)}, u32[]{:S(2)}) %collective-permute-start.2) | collective-permute-done | bytes 1048608 | tf_op jit(solution)/shard_map/ppermute | solution.py:15
  33.6 24.7 %collective-permute-done.1 = bf16[256,2048]{1,0:T(8,128)(2,1)} collective-permute-done((bf16[256,2048]{1,0:T(8,128)(2,1)S(1)}, bf16[256,2048]{1,0:T(8,128)(2,1)}, u32[]{:S(2)}, u32[]{:S(2)}) %collective-permute-start.1) | collective-permute-done | bytes 1048608 | tf_op jit(solution)/shard_map/ppermute | solution.py:15
  58.3 1.8 pad_maximum_fusion
  64.9 0.9 fusion.33
  65.8 1.4 multiply_reduce_fusion.1
  67.2 1.1 multiply_reduce_fusion.3
  68.3 1.1 multiply_reduce_fusion.2
  69.4 1.0 multiply_convert_fusion.6
  71.9 1.0 multiply_convert_fusion.1
  72.9 1.2 multiply_convert_fusion.3
  75.7 0.6 convolution_dynamic-update-slice_fusion.7
  76.9 0.6 convolution_dynamic-update-slice_fusion.5
  77.5 0.6 convolution_dynamic-update-slice_fusion.4
  79.3 0.6 convolution_dynamic-update-slice_fusion.1
  80.0 0.6 convolution_dynamic-update-slice_fusion
  81.1 1.3 collective-permute-start.4
  82.4 1.3 collective-permute-start.3
  85.6 29.1 %collective-permute-done.4 = f32[256,2048]{1,0:T(8,128)S(1)} collective-permute-done((f32[256,2048]{1,0:T(8,128)S(1)}, f32[256,2048]{1,0:T(8,128)S(1)}, u32[]{:S(2)}, u32[]{:S(2)}) %collective-permute-start.4) | collective-permute-done | bytes 2097184 | tf_op jit(solution)/shard_map/ppermute | solution.py:15
  114.7 46.9 %collective-permute-done.3 = f32[256,2048]{1,0:T(8,128)S(1)} collective-permute-done((f32[256,2048]{1,0:T(8,128)S(1)}, f32[256,2048]{1,0:T(8,128)S(1)}, u32[]{:S(2)}, u32[]{:S(2)}) %collective-permute-start.3) | collective-permute-done | bytes 2097184 | tf_op jit(solution)/shard_map/ppermute | solution.py:15
  161.7 0.6 constant_dynamic-update-slice_fusion.8
  162.7 1.3 collective-permute-start.5
  164.5 44.3 %collective-permute-done.5 = f32[1,3072]{1,0:T(1,128)S(1)} collective-permute-done((f32[1,3072]{1,0:T(1,128)S(1)}, f32[1,3072]{1,0:T(1,128)S(1)}, u32[]{:S(2)}, u32[]{:S(2)}) %collective-permute-start.5) | collective-permute-done | bytes 12320 | tf_op jit(solution)/shard_map/ppermute | solution.py:15
  208.9 2.2 multiply_reduce_fusion
  211.1 137.2 %psum.7 = f32[3072]{0:T(1024)S(1)} all-reduce(f32[3072]{0:T(1024)S(1)} %get-tuple-element.20), channel_id=1, replica_groups=mesh['seq'=128,'dp'=4] {'seq','dp'}, use_global_device_ids=true, to_apply=%region_27.28 | all-reduce | flops 3072 | bytes 24576 | tf_op jit(solution)/shard_map/psum | solution.py:124
  (60 shorter events, 13.5 us)
Async XLA Ops:
  5.4 4.9 %collective-permute-start = (bf16[1,3072]{1,0:T(2,128)(2,1)S(1)}, bf16[1,3072]{1,0:T(2,128)(2,1)S(1)}, u32[]{:S(2)}, u32[]{:S(2)}) collective-permute-start(bf16[1,3072]{1,0:T(2,128)(2,1)S(1)} %dynamic-slice_bitcast_fusion), channel_id=1, source_target_pairs={{0,4},{4,8},{8,12},{12,16},{16,20},{20,24},{24,28},{28,32},{32,36}... | collective-permute-start | bytes 18440 | tf_op jit(solution)/shard_map/ppermute | solution.py:15
  12.6 21.1 %collective-permute-start.2 = (bf16[256,2048]{1,0:T(8,128)(2,1)S(1)}, bf16[256,2048]{1,0:T(8,128)(2,1)}, u32[]{:S(2)}, u32[]{:S(2)}) collective-permute-start(bf16[256,2048]{1,0:T(8,128)(2,1)S(1)} %slice.154), channel_id=1, source_target_pairs={{0,4},{4,8},{8,12},{12,16},{16,20},{20,24},{24,28},{28,32},{32,36}... | collective-permute-start | bytes 3145736 | tf_op jit(solution)/shard_map/ppermute | solution.py:15
  17.2 41.1 %collective-permute-start.1 = (bf16[256,2048]{1,0:T(8,128)(2,1)S(1)}, bf16[256,2048]{1,0:T(8,128)(2,1)}, u32[]{:S(2)}, u32[]{:S(2)}) collective-permute-start(bf16[256,2048]{1,0:T(8,128)(2,1)S(1)} %slice.154), channel_id=1, source_target_pairs={{0,8},{4,12},{8,16},{12,20},{16,24},{20,28},{24,32},{28,36},{32,40... | collective-permute-start | bytes 3145736 | tf_op jit(solution)/shard_map/ppermute | solution.py:15
  62.0 1.8 copy-start.1
  81.1 33.7 %collective-permute-start.4 = (f32[256,2048]{1,0:T(8,128)S(1)}, f32[256,2048]{1,0:T(8,128)S(1)}, u32[]{:S(2)}, u32[]{:S(2)}) collective-permute-start(f32[256,2048]{1,0:T(8,128)S(1)} %get-tuple-element.19), channel_id=1, source_target_pairs={{8,0},{12,4},{16,8},{20,12},{24,16},{28,20},{32,24},{36,28},{40,32... | collective-permute-start | bytes 6291464 | tf_op jit(solution)/shard_map/ppermute | solution.py:15
  82.4 79.3 %collective-permute-start.3 = (f32[256,2048]{1,0:T(8,128)S(1)}, f32[256,2048]{1,0:T(8,128)S(1)}, u32[]{:S(2)}, u32[]{:S(2)}) collective-permute-start(f32[256,2048]{1,0:T(8,128)S(1)} %get-tuple-element.18), channel_id=1, source_target_pairs={{4,0},{8,4},{12,8},{16,12},{20,16},{24,20},{28,24},{32,28},{36,32}... | collective-permute-start | bytes 6291464 | tf_op jit(solution)/shard_map/ppermute | solution.py:15
  162.7 46.1 %collective-permute-start.5 = (f32[1,3072]{1,0:T(1,128)S(1)}, f32[1,3072]{1,0:T(1,128)S(1)}, u32[]{:S(2)}, u32[]{:S(2)}) collective-permute-start(f32[1,3072]{1,0:T(1,128)S(1)} %bitcast.89), channel_id=1, source_target_pairs={{4,0},{8,4},{12,8},{16,12},{20,16},{24,20},{28,24},{32,28},{36,32}... | collective-permute-start | bytes 36872 | tf_op jit(solution)/shard_map/ppermute | solution.py:15
  164.0 44.8 %copy-start = (bf16[1,64,3072]{2,1,0:T(8,128)(2,1)S(1)}, bf16[1,64,3072]{2,1,0:T(8,128)(2,1)}, u32[]{:S(2)}) copy-start(bf16[1,64,3072]{2,1,0:T(8,128)(2,1)} %param.7) | copy-start | bytes 1179652
  164.1 44.8 %copy-start.2 = (f32[3072]{0:T(1024)S(1)}, f32[3072]{0:T(1024)}, u32[]{:S(2)}) copy-start(f32[3072]{0:T(1024)} %param.8) | copy-start | bytes 36868
  164.1 44.8 %copy-start.3 = (s32[1,256]{1,0:T(1,128)S(1)}, s32[1,256]{1,0:T(1,128)}, u32[]{:S(2)}) copy-start(s32[1,256]{1,0:T(1,128)} %param.10) | copy-start | bytes 3076
  164.5 46.6 %copy-start.4 = (bf16[1,256,3072]{2,1,0:T(8,128)(2,1)}, bf16[1,256,3072]{2,1,0:T(8,128)(2,1)S(1)}, u32[]{:S(2)}) copy-start(bf16[1,256,3072]{2,1,0:T(8,128)(2,1)S(1)} %bitcast_dynamic-update-slice_fusion) | copy-start | bytes 4718596
where the time goes:
time: 349 us
  waiting for transfers between devices  157 us (45%)
  blocking collectives  137 us (39%)
  matrix products  23.3 us (7%)
  starting transfers between devices  17.6 us (5%)
  other arithmetic  9.05 us (3%)
  between operations  3.69 us (1%)
    ppermute x6, waiting for transfers between devices, shifted(): lax.ppermute(value, axis, [(source, source + steps) for source in range(i...  157 us
    psum x1, blocking collectives, local(): gain_grad = lax.psum(gain_term, ('seq', 'dp')) / row_count  137 us
    ppermute x6, starting transfers between devices, shifted(): lax.ppermute(value, axis, [(source, source + steps) for source in range(i...  17.6 us
  transfers between devices with their start and end apart: 6, of which 6 were waited for; matrix products, arithmetic and copies ran while one was open for 1% of the time, Pallas kernels for 0%

commit v1 on v0

--- a/solution.py
+++ b/solution.py
@@ -121,7 +121,7 @@
     slot_sums = slot_sums + (slot_index == last_slot).astype(jnp.float32) * from_next
     patch_grad = (patch_gain * slot_sums).astype(jnp.bfloat16)[None]
     gain_term = jnp.sum(slot_sums * patch_table.astype(jnp.float32), axis=0)
-    gain_grad = lax.psum(gain_term, ("seq", "dp")) / row_count
+    gain_grad = lax.psum(lax.psum(gain_term, "dp"), "seq") / row_count
     return (byte_grad, patch_grad, gain_grad)
 
 

time: 349 us -> 983 us (2.82)
  the two profiles are of different devices: /device:TPU:1 before, /device:TPU:0 now
where the time goes in v1:
time: 983 us; the launch traced here: 982 us
  blocking collectives  755 us (77%)
  waiting for transfers between devices  178 us (18%)
  matrix products  23.1 us (2%)
  starting transfers between devices  12.7 us (1%)
    psum x2, blocking collectives, local(): gain_grad = lax.psum(lax.psum(gain_term, 'dp'), 'seq') / row_count  755 us
    ppermute x6, waiting for transfers between devices, shifted(): lax.ppermute(value, axis, [(source, source + steps) for source in range(i...  178 us
  transfers between devices with their start and end apart: 6, of which 5 were waited for; matrix products, arithmetic and copies ran while one was open for 0% of the time, Pallas kernels for 0%

profile of v1, /device:TPU:0, one launch (start us, length us, event | category | flops | bytes accessed | tf_op | source)
XLA Modules:
  0.0 982.3 jit_solution(3522328260849888870)
XLA Ops:
  1.3 1.3 select_reduce_fusion.1
  4.5 0.8 dynamic-slice_bitcast_fusion
  5.4 1.3 collective-permute-start
  6.7 1.4 collective-permute-done
  8.1 2.3 fusion
  10.4 5.2 collective-permute-start.2
  15.6 2.3 collective-permute-start.1
  17.9 0.6 compare_convert_fusion
  18.7 20.7 %collective-permute-done.2 = bf16[256,2048]{1,0:T(8,128)(2,1)} collective-permute-done((bf16[256,2048]{1,0:T(8,128)(2,1)S(1)}, bf16[256,2048]{1,0:T(8,128)(2,1)}, u32[]{:S(2)}, u32[]{:S(2)}) %collective-permute-start.2) | collective-permute-done | bytes 1048608 | tf_op jit(solution)/shard_map/ppermute | solution.py:15
  39.4 18.0 %collective-permute-done.1 = bf16[256,2048]{1,0:T(8,128)(2,1)} collective-permute-done((bf16[256,2048]{1,0:T(8,128)(2,1)S(1)}, bf16[256,2048]{1,0:T(8,128)(2,1)}, u32[]{:S(2)}, u32[]{:S(2)}) %collective-permute-start.1) | collective-permute-done | bytes 1048608 | tf_op jit(solution)/shard_map/ppermute | solution.py:15
  57.4 1.7 pad_maximum_fusion
  63.9 0.9 fusion.33
  64.8 1.4 multiply_reduce_fusion.1
  66.1 1.0 multiply_reduce_fusion.3
  67.1 1.0 multiply_reduce_fusion.2
  68.2 1.0 multiply_convert_fusion.6
  70.7 0.9 multiply_convert_fusion.1
  71.6 1.2 multiply_convert_fusion.3
  74.4 0.6 convolution_dynamic-update-slice_fusion.7
  75.0 0.6 convolution_dynamic-update-slice_fusion.6
  76.2 0.6 convolution_dynamic-update-slice_fusion.4
  76.8 0.6 convolution_dynamic-update-slice_fusion.3
  77.4 0.6 convolution_dynamic-update-slice_fusion.2
  79.8 1.3 collective-permute-start.4
  81.1 1.3 collective-permute-start.3
  84.3 112.4 %collective-permute-done.4 = f32[256,2048]{1,0:T(8,128)S(1)} collective-permute-done((f32[256,2048]{1,0:T(8,128)S(1)}, f32[256,2048]{1,0:T(8,128)S(1)}, u32[]{:S(2)}, u32[]{:S(2)}) %collective-permute-start.4) | collective-permute-done | bytes 2097184 | tf_op jit(solution)/shard_map/ppermute | solution.py:15
  196.7 0.6 constant_dynamic-update-slice_fusion.8
  197.7 1.3 collective-permute-start.5
  199.5 25.3 %collective-permute-done.5 = f32[1,3072]{1,0:T(1,128)S(1)} collective-permute-done((f32[1,3072]{1,0:T(1,128)S(1)}, f32[1,3072]{1,0:T(1,128)S(1)}, u32[]{:S(2)}, u32[]{:S(2)}) %collective-permute-start.5) | collective-permute-done | bytes 12320 | tf_op jit(solution)/shard_map/ppermute | solution.py:15
  224.8 2.2 multiply_reduce_fusion
  227.1 19.8 %psum.14 = f32[3072]{0:T(1024)S(1)} all-reduce(f32[3072]{0:T(1024)S(1)} %get-tuple-element.20), channel_id=1, replica_groups=mesh['seq'=128,'dp'=4] {'dp'}, use_global_device_ids=true, to_apply=%region_27.28 | all-reduce | flops 3072 | bytes 24576 | tf_op jit(solution)/shard_map/psum | solution.py:124
  246.9 734.8 %psum.15 = f32[3072]{0:T(1024)S(1)} all-reduce(f32[3072]{0:T(1024)S(1)} %psum.14), channel_id=1, replica_groups=mesh['seq'=128,'dp'=4] {'seq'}, use_global_device_ids=true, to_apply=%region_28.29 | all-reduce | flops 3072 | bytes 24576 | tf_op jit(solution)/shard_map/psum | solution.py:124
  (61 shorter events, 13.4 us)
Async XLA Ops:
  5.4 2.7 collective-permute-start
  10.4 29.0 %collective-permute-start.2 = (bf16[256,2048]{1,0:T(8,128)(2,1)S(1)}, bf16[256,2048]{1,0:T(8,128)(2,1)}, u32[]{:S(2)}, u32[]{:S(2)}) collective-permute-start(bf16[256,2048]{1,0:T(8,128)(2,1)S(1)} %slice.154), channel_id=1, source_target_pairs={{0,4},{4,8},{8,12},{12,16},{16,20},{20,24},{24,28},{28,32},{32,36}... | collective-permute-start | bytes 3145736 | tf_op jit(solution)/shard_map/ppermute | solution.py:15
  15.6 41.8 %collective-permute-start.1 = (bf16[256,2048]{1,0:T(8,128)(2,1)S(1)}, bf16[256,2048]{1,0:T(8,128)(2,1)}, u32[]{:S(2)}, u32[]{:S(2)}) collective-permute-start(bf16[256,2048]{1,0:T(8,128)(2,1)S(1)} %slice.154), channel_id=1, source_target_pairs={{0,8},{4,12},{8,16},{12,20},{16,24},{20,28},{24,32},{28,36},{32,40... | collective-permute-start | bytes 3145736 | tf_op jit(solution)/shard_map/ppermute | solution.py:15
  60.9 1.8 copy-start.1
  79.8 116.9 %collective-permute-start.4 = (f32[256,2048]{1,0:T(8,128)S(1)}, f32[256,2048]{1,0:T(8,128)S(1)}, u32[]{:S(2)}, u32[]{:S(2)}) collective-permute-start(f32[256,2048]{1,0:T(8,128)S(1)} %get-tuple-element.19), channel_id=1, source_target_pairs={{8,0},{12,4},{16,8},{20,12},{24,16},{28,20},{32,24},{36,28},{40,32... | collective-permute-start | bytes 6291464 | tf_op jit(solution)/shard_map/ppermute | solution.py:15
  81.1 115.6 %collective-permute-start.3 = (f32[256,2048]{1,0:T(8,128)S(1)}, f32[256,2048]{1,0:T(8,128)S(1)}, u32[]{:S(2)}, u32[]{:S(2)}) collective-permute-start(f32[256,2048]{1,0:T(8,128)S(1)} %get-tuple-element.18), channel_id=1, source_target_pairs={{4,0},{8,4},{12,8},{16,12},{20,16},{24,20},{28,24},{32,28},{36,32}... | collective-permute-start | bytes 6291464 | tf_op jit(solution)/shard_map/ppermute | solution.py:15
  197.7 27.1 %collective-permute-start.5 = (f32[1,3072]{1,0:T(1,128)S(1)}, f32[1,3072]{1,0:T(1,128)S(1)}, u32[]{:S(2)}, u32[]{:S(2)}) collective-permute-start(f32[1,3072]{1,0:T(1,128)S(1)} %bitcast.89), channel_id=1, source_target_pairs={{4,0},{8,4},{12,8},{16,12},{20,16},{24,20},{28,24},{32,28},{36,32}... | collective-permute-start | bytes 36872 | tf_op jit(solution)/shard_map/ppermute | solution.py:15
  199.0 25.8 %copy-start = (bf16[1,64,3072]{2,1,0:T(8,128)(2,1)S(1)}, bf16[1,64,3072]{2,1,0:T(8,128)(2,1)}, u32[]{:S(2)}) copy-start(bf16[1,64,3072]{2,1,0:T(8,128)(2,1)} %param.7) | copy-start | bytes 1179652
  199.0 25.8 %copy-start.2 = (f32[3072]{0:T(1024)S(1)}, f32[3072]{0:T(1024)}, u32[]{:S(2)}) copy-start(f32[3072]{0:T(1024)} %param.8) | copy-start | bytes 36868
  199.1 25.8 %copy-start.3 = (s32[1,256]{1,0:T(1,128)S(1)}, s32[1,256]{1,0:T(1,128)}, u32[]{:S(2)}) copy-start(s32[1,256]{1,0:T(1,128)} %param.10) | copy-start | bytes 3076
  199.5 27.5 %copy-start.4 = (bf16[1,256,3072]{2,1,0:T(8,128)(2,1)}, bf16[1,256,3072]{2,1,0:T(8,128)(2,1)S(1)}, u32[]{:S(2)}) copy-start(bf16[1,256,3072]{2,1,0:T(8,128)(2,1)S(1)} %bitcast_dynamic-update-slice_fusion) | copy-start | bytes 4718596
